TPU v7x, 32 devices: a whole 2x2x4 slice. The times are simulated.
32 devices in a mesh: groups: 2 (over y), mp: 4 (over z), batch: 2 (over x), rep: 2 (over core).
Axes of the slice: x: 2, y: 2, z: 4, core: 2. Of those that a mesh axis runs over, the one named last changes fastest.
Arguments:
- attention_input: bfloat16 [1024, 8192], P(('groups', 'batch'), 'mp'), parts along dimension 0, may hold values from -6 to 6
- output_weight_matrix: bfloat16 [8192, 8192], P('mp', 'rep'), may hold values from -0.09375 to 0.09375
- down_factor_weights: bfloat16 [64, 8192, 64], P('batch', 'mp'), may hold values from -0.0625 to 0.0625
- up_factor_weights: bfloat16 [64, 64, 8192], P('batch', None, ('rep', 'mp')), may hold values from -0.75 to 0.75
- adapter_request_lists: int32 [4, 2, 4], P('groups'), parts along dimension 0, may hold values from 0 to 31, as said below
- request_adapter_slot: int32 [1024], P(('groups', 'batch')), parts along dimension 0, may hold values from 0 to 7, as said below
Outputs:
- projected: bfloat16 [1024, 8192], P(('groups', 'batch'), ('rep', 'mp')), parts along dimension 0
There are 2 independent parts, one for each index of `groups`. A program takes and returns all parts, laid end to end along the dimension named above; an argument that names none is the same for every part. Nothing has to cross between parts.
Inputs may be any that keep to these rules, and one draw needn't show every extreme that they name: Each entry adapter_request_lists[b, h] holds 4 distinct numbers. `request_adapter_slot`: every slot appears among the requests of each index of batch.
All inputs are finite; a program needn't handle non-finite values.
Results may differ from a plain program's by a relative error of at most 0.0024.
Values may be sent and summed in bfloat16 or wider, within the bound.
A program may use at most 128 MiB of HBM per device.

v0:
```python
import jax
import jax.numpy as jnp
from jax import lax
from jax.sharding import PartitionSpec as P


def per_device(
    attention_input,
    output_weight_matrix,
    down_factor_weights,
    up_factor_weights,
    adapter_request_lists,
    request_adapter_slot,
):
    my_index = lax.axis_index("batch")
    wanted = adapter_request_lists[:, my_index, :]
    picked_down = down_factor_weights[wanted]
    picked_up = up_factor_weights[wanted]
    got_down, got_up = (
        lax.all_to_all(picked_down, "batch", split_axis=0, concat_axis=0, tiled=True),
        lax.all_to_all(picked_up, "batch", split_axis=0, concat_axis=0, tiled=True),
    )
    table_down = got_down.reshape((-1,) + down_factor_weights.shape[1:])
    table_up = got_up.reshape((-1,) + up_factor_weights.shape[1:])
    slots = table_down.shape[0]
    base = jnp.dot(attention_input, output_weight_matrix, preferred_element_type=jnp.float32)
    selector = (
        request_adapter_slot[:, None] == jnp.arange(slots, dtype=jnp.int32)[None, :]
    ).astype(jnp.float32)
    every_slot = jnp.einsum(
        "tk,nkr->tnr", attention_input, table_down, preferred_element_type=jnp.float32
    )
    partial_shrink = jnp.einsum("tn,tnr->tr", selector, every_slot)
    shrink = lax.psum(partial_shrink, "mp").astype(jnp.bfloat16)
    spread = (selector.astype(jnp.bfloat16)[:, :, None] * shrink[:, None, :]).reshape(
        shrink.shape[0], -1
    )
    expand = jnp.dot(
        spread, table_up.reshape(-1, table_up.shape[2]), preferred_element_type=jnp.float32
    )
    summed = lax.psum_scatter(base, "mp", scatter_dimension=1, tiled=True)
    return (summed + 0.5 * expand).astype(jnp.bfloat16)


def solution(mesh):
    in_specs = (
        P(("groups", "batch"), "mp"),
        P("mp", "rep"),
        P("batch", "mp", None),
        P("batch", None, ("rep", "mp")),
        P("groups", None, None),
        P(("groups", "batch")),
    )
    out_specs = P(("groups", "batch"), ("rep", "mp"))
    return jax.shard_map(
        per_device, mesh=mesh, in_specs=in_specs, out_specs=out_specs, check_vma=False
    )
```

profile of v0, /device:TPU:0, one launch (start us, length us, event | category | flops | bytes accessed | tf_op | source)
XLA Modules:
  0.0 108.9 jit_solution(16173496047814000953)
XLA Ops:
  6.5 0.0 copy-start
  6.5 0.0 reduce-scatter.2.cloned.1.call-start
  6.5 1.2 %copy-done = bf16[256,2048]{1,0:T(8,128)(2,1)S(1)} copy-done((bf16[256,2048]{1,0:T(8,128)(2,1)S(1)}, bf16[256,2048]{1,0:T(8,128)(2,1)}, u32[]{:S(2)}) %copy-start) | copy-done | bytes 1048600
  7.8 10.1 %fusion.7 = f32[256,4096]{1,0:T(8,128)} fusion(bf16[256,2048]{1,0:T(8,128)(2,1)S(1)} %copy-done, bf16[2048,4096]{1,0:T(8,128)(2,1)} %param.7), kind=kOutput, calls=%fused_computation.16 | convolution fusion | flops 4294967296 | bytes 22020096 | tf_op jit(solution)/shard_map/dot_general | solution.py:26
  17.8 0.0 copy-start.3
  17.8 0.0 reduce-scatter.2.cloned.1.call-update
  17.9 0.7 copy-done.3
  18.5 0.1 reshape.71
  18.6 5.4 %gather_fusion = bf16[8,2048,64]{1,2,0:T(8,128)(2,1)} fusion(bf16[32,2048,64]{1,2,0:T(8,128)(2,1)} %param.8, s32[1024]{0:T(1024)S(1)} %pad_clamp_fusion), kind=kCustom, calls=%fused_computation | custom fusion | bytes 4194336 | tf_op jit(solution)/shard_map/gather | solution.py:17
  24.0 0.0 copy-start.2
  24.0 4.3 %all-to-all-start = ((bf16[2,4,2048,64]{2,3,1,0:T(8,128)(2,1)}), bf16[2,4,2048,64]{2,3,1,0:T(8,128)(2,1)S(1)}, u32[]{:S(2)}, u32[]{:S(2)}) async-start(bf16[2,4,2048,64]{2,3,1,0:T(8,128)(2,1)} %bitcast.1), calls=%async_computation.1 | async-start | bytes 4194304 | tf_op jit(solution)/shard_map/all_to_all | solution.py:20
  28.3 3.8 %gather_fusion.1 = bf16[8,64,1024]{2,1,0:T(8,128)(2,1)} fusion(bf16[32,64,1024]{2,1,0:T(8,128)(2,1)} %param.9, s32[1024]{0:T(1024)S(1)} %pad_clamp_fusion), kind=kCustom, calls=%fused_computation.1 | custom fusion | bytes 2097184 | tf_op jit(solution)/shard_map/gather | solution.py:18
  32.1 0.0 copy-done.2
  32.1 22.3 %all-to-all-done = bf16[2,4,2048,64]{2,3,1,0:T(8,128)(2,1)S(1)} async-done(((bf16[2,4,2048,64]{2,3,1,0:T(8,128)(2,1)}), bf16[2,4,2048,64]{2,3,1,0:T(8,128)(2,1)S(1)}, u32[]{:S(2)}, u32[]{:S(2)}) %all-to-all-start) | async-done | bytes 2097184 | tf_op jit(solution)/shard_map/all_to_all | solution.py:20
  54.4 0.0 copy-start.1
  54.4 1.3 %copy-done.1 = bf16[2,4,2048,64]{2,3,1,0:T(8,128)(2,1)} copy-done((bf16[2,4,2048,64]{2,3,1,0:T(8,128)(2,1)}, bf16[2,4,2048,64]{2,3,1,0:T(8,128)(2,1)S(1)}, u32[]{:S(2)}) %copy-start.1) | copy-done | bytes 2097176
  55.7 3.6 %all-to-all-start.1 = ((bf16[2,4,64,1024]{3,2,1,0:T(8,128)(2,1)}), bf16[2,4,64,1024]{3,2,1,0:T(8,128)(2,1)S(1)}, u32[]{:S(2)}, u32[]{:S(2)}) async-start(bf16[2,4,64,1024]{3,2,1,0:T(8,128)(2,1)} %bitcast.6), calls=%async_computation.2 | async-start | bytes 2097152 | tf_op jit(solution)/shard_map/all_to_all | solution.py:21
  59.3 2.3 %fusion.3 = f32[256,64]{0,1:T(8,128)S(1)} fusion(bf16[8,2048,64]{1,2,0:T(8,128)(2,1)} %bitcast.23, bf16[256,2048]{1,0:T(8,128)(2,1)S(1)} %copy-done, f32[256,8]{0,1:T(8,128)S(1)} %get-tuple-element.6), kind=kOutput, calls=%fused_computation.7 | convolution fusion | flops 537116672 | bytes 3219456 | tf_op jit(solution)/shard_map/tk,nkr->tnr/dot_general | solution.py:30
  61.6 24.9 %psum.7 = bf16[256,64]{0,1:T(8,128)(2,1)S(1)} all-reduce(f32[256,64]{0,1:T(8,128)S(1)} %fusion.3), channel_id=1, replica_groups=mesh['groups'=2,'mp'=4,'batch'=2,'rep'=2] {'mp'}, use_global_device_ids=true, to_apply=%region_1.0 | all-reduce | flops 16384 | bytes 98304 | tf_op jit(solution)/shard_map/psum | solution.py:34
  86.6 0.0 all-to-all-done.1
  86.6 13.0 %reduce-scatter.2.cloned.1.call-done = f32[256,1024]{1,0:T(8,128)} async-done(((f32[256,4096]{1,0:T(8,128)}), f32[256,1024]{1,0:T(8,128)}) %reduce-scatter.2.cloned.1.call-update) | async-done | bytes 1048592 | tf_op jit(solution)/shard_map/reduce_scatter | solution.py:41
  99.6 2.5 %fusion.1 = bf16[256,1024]{1,0:T(8,128)(2,1)} fusion(f32[256,1024]{1,0:T(8,128)} %reduce-scatter.2.cloned.1.call-done, bf16[256,512]{0,1:T(8,128)(2,1)S(1)} %bitcast.24, bf16[512,1024]{1,0:T(8,128)(2,1)S(1)} %bitcast.22), kind=kOutput, calls=%fused_computation.4 | convolution fusion | flops 269221888 | bytes 2883584 | tf_op jit(solution)/shard_map/dot_general | solution.py:38
  (5 shorter events, 0.0 us)
Async XLA Ops:
  6.5 1.2 %copy-start = (bf16[256,2048]{1,0:T(8,128)(2,1)S(1)}, bf16[256,2048]{1,0:T(8,128)(2,1)}, u32[]{:S(2)}) copy-start(bf16[256,2048]{1,0:T(8,128)(2,1)} %param.6) | copy-start | bytes 3145732
  6.5 93.0 %reduce-scatter.2.cloned.1.call-start = ((), (), s32[]{:S(2)}) async-start(), calls=%async_computation.3 | async-start | bytes 5242880 | tf_op jit(solution)/shard_map/reduce_scatter | solution.py:41
  17.8 0.7 copy-start.3
  24.0 8.1 %copy-start.2 = (s32[256]{0:T(256)S(1)}, s32[256]{0:T(256)}, u32[]{:S(2)}) copy-start(s32[256]{0:T(256)} %param.11) | copy-start | bytes 3076
  24.0 30.4 %all-to-all-start = ((bf16[2,4,2048,64]{2,3,1,0:T(8,128)(2,1)}), bf16[2,4,2048,64]{2,3,1,0:T(8,128)(2,1)S(1)}, u32[]{:S(2)}, u32[]{:S(2)}) async-start(bf16[2,4,2048,64]{2,3,1,0:T(8,128)(2,1)} %bitcast.1), calls=%async_computation.1 | async-start | bytes 4194304 | tf_op jit(solution)/shard_map/all_to_all | solution.py:20
  54.4 1.3 %copy-start.1 = (bf16[2,4,2048,64]{2,3,1,0:T(8,128)(2,1)}, bf16[2,4,2048,64]{2,3,1,0:T(8,128)(2,1)S(1)}, u32[]{:S(2)}) copy-start(bf16[2,4,2048,64]{2,3,1,0:T(8,128)(2,1)S(1)} %all-to-all-done) | copy-start | bytes 6291460
  55.7 30.9 %all-to-all-start.1 = ((bf16[2,4,64,1024]{3,2,1,0:T(8,128)(2,1)}), bf16[2,4,64,1024]{3,2,1,0:T(8,128)(2,1)S(1)}, u32[]{:S(2)}, u32[]{:S(2)}) async-start(bf16[2,4,64,1024]{3,2,1,0:T(8,128)(2,1)} %bitcast.6), calls=%async_computation.2 | async-start | bytes 2097152 | tf_op jit(solution)/shard_map/all_to_all | solution.py:21
Sparse Core Ops, SparseCore 0:
  18.0 81.5 reduce-scatter.1
where the time goes:
time: 109 us
  waiting for transfers between devices  35.3 us (32%)
  blocking collectives  24.9 us (23%)
  matrix products  14.9 us (14%)
  between operations  13.4 us (12%)
  local copies, waits for them, and re-layouts  12.4 us (11%)
  starting transfers between devices  7.92 us (7%)
    psum x1, blocking collectives, per_device(): shrink = lax.psum(partial_shrink, 'mp').astype(jnp.bfloat16)  24.9 us
    all_to_all x1, waiting for transfers between devices, per_device(): lax.all_to_all(picked_down, 'batch', split_axis=0, concat_axis=0, tiled=T...  22.3 us
    reduce_scatter x1, waiting for transfers between devices, per_device(): summed = lax.psum_scatter(base, 'mp', scatter_dimension=1, tiled=True)  13 us
    dot_general x1, matrix products, per_device(): jnp.dot(attention_input, output_weight_matrix, preferred_element_type=jnp...  10.1 us
    gather x1, local copies, waits for them, and re-layouts, per_device(): picked_down = down_factor_weights[wanted]  5.37 us
    all_to_all x1, starting transfers between devices, per_device(): lax.all_to_all(picked_down, 'batch', split_axis=0, concat_axis=0, tiled=T...  4.34 us
    gather x1, local copies, waits for them, and re-layouts, per_device(): picked_up = up_factor_weights[wanted]  3.8 us
    all_to_all x1, starting transfers between devices, per_device(): lax.all_to_all(picked_up, 'batch', split_axis=0, concat_axis=0, tiled=True)  3.58 us
  transfers between devices with their start and end apart: 3, of which 2 were waited for; matrix products, arithmetic and copies ran while one was open for 11% of the time, Pallas kernels for 0%

commit v1 on v0

v1 whole, which is shorter than its diff:
```python
import functools

import jax
import jax.numpy as jnp
from jax import lax
from jax.experimental import pallas as pl
from jax.experimental.pallas import tpu as pltpu
from jax.sharding import PartitionSpec as P

MESH = pl.DeviceIdType.MESH
TOP = 32766.0
DEPTH = 2
AHEAD = 2


def kernel(
    n, reps, nb, cw,
    x_hbm, w_hbm, a_hbm, b_hbm, lists, slot_ref, out_ref,
    x_v, w_v, a_all, b_all, a_snd, a_tab, b_snd, b_tab,
    snd, snd_scale, rcv, rcv_scale, rs_snd, rs_rcv, ag, spread, acc,
    x_sem, w_sem, ab_sem, snd_sem, snd_scale_sem, rcv_sem, rcv_scale_sem,
    xs_sem, xr_sem, small_sem,
):
    me, rep, mine = lax.axis_index("mp"), lax.axis_index("rep"), lax.axis_index("batch")
    chunks = acc.shape[0]
    steps = (n - 1) * chunks
    cap = lists.shape[2]
    half = cap // reps
    rank = a_tab.shape[2]
    nd = n * reps
    lin = me * reps + rep
    counts = ((n - 1 - me) * chunks, me * chunks)

    def w_copy(q):
        return pltpu.make_async_copy(
            w_hbm.at[:, pl.ds(pl.multiple_of(q * cw, cw), cw)], w_v.at[q], w_sem.at[q]
        )

    def chunk_of(t, d):
        s, c = t // chunks, t % chunks
        return ((n - 1 - s) if d == 0 else s) * chunks + c

    def fetch(t):
        for d in range(2):
            @pl.when(t < counts[d])
            def _():
                w_copy(chunk_of(t, d)).start()

    x_copy = pltpu.make_async_copy(x_hbm, x_v, x_sem)
    a_copy = pltpu.make_async_copy(a_hbm, a_all, ab_sem.at[0])
    b_copy = pltpu.make_async_copy(b_hbm, b_all, ab_sem.at[1])
    x_copy.start()
    for t in range(AHEAD):
        fetch(t)
    a_copy.start()

    barrier = pltpu.get_barrier_semaphore()

    def peer(k):
        p = lax.rem(lin + k, nd)
        return p, {"mp": p // reps, "rep": lax.rem(p, reps)}

    for k in range(1, nb):
        pl.semaphore_signal(
            barrier, inc=1, device_id={"batch": lax.rem(mine + k, nb)}, device_id_type=MESH
        )

    def greet(k, carry):
        pl.semaphore_signal(barrier, inc=1, device_id=peer(k)[1], device_id_type=MESH)
        return carry

    lax.fori_loop(1, nd, greet, 0)
    pl.semaphore_wait(barrier, nd - 1 + nb - 1)
    x_copy.wait()

    def sends(t, d):
        to = {"mp": me + 1 if d == 0 else me - 1}
        return (
            pltpu.make_async_remote_copy(
                snd.at[d, t % DEPTH], rcv.at[d, t], snd_sem.at[d, t % DEPTH],
                rcv_sem.at[d, t], device_id=to, device_id_type=MESH,
            ),
            pltpu.make_async_remote_copy(
                snd_scale.at[d, t % DEPTH], rcv_scale.at[d, t], snd_scale_sem.at[d, t % DEPTH],
                rcv_scale_sem.at[d, t], device_id=to, device_id_type=MESH,
            ),
        )

    def a_send(k):
        return pltpu.make_async_remote_copy(
            a_snd.at[k - 1], a_tab.at[mine], xs_sem.at[0, k - 1], xr_sem.at[0, k - 1],
            device_id={"batch": lax.rem(mine + k, nb)}, device_id_type=MESH,
        )

    def b_send(k):
        return pltpu.make_async_remote_copy(
            b_snd.at[k - 1], b_tab.at[mine], xs_sem.at[1, k - 1], xr_sem.at[1, k - 1],
            device_id={"batch": lax.rem(mine + k, nb)}, device_id_type=MESH,
        )

    def rs_send(k):
        p, to = peer(k)
        return pltpu.make_async_remote_copy(
            rs_snd.at[p], rs_rcv.at[k - 1], small_sem.at[0], small_sem.at[1],
            device_id=to, device_id_type=MESH,
        )

    def ag_send(k):
        return pltpu.make_async_remote_copy(
            ag.at[lin], ag.at[lin], small_sem.at[2], small_sem.at[3],
            device_id=peer(k)[1], device_id_type=MESH,
        )

    def all_small(buf, i):
        part = buf.at[pl.ds(0, nd - 1)]
        return pltpu.make_async_remote_copy(
            part, part, small_sem.at[i], small_sem.at[i + 1],
            device_id=peer(1)[1], device_id_type=MESH,
        )

    def pick_down():
        a_copy.wait()
        for k in range(1, nb):
            to = lax.rem(mine + k, nb)
            for j in range(half):
                a_snd[k - 1, j] = a_all[lists[to, mine, rep * half + j]]
            a_send(k).start()
        for j in range(half):
            a_tab[mine, j] = a_all[lists[mine, mine, rep * half + j]]

    def pick_up():
        b_copy.wait()
        for k in range(1, nb):
            to = lax.rem(mine + k, nb)
            for j in range(cap):
                b_snd[k - 1, j] = b_all[lists[to, mine, j]]
            b_send(k).start()
        for j in range(cap):
            b_tab[mine, j] = b_all[lists[mine, mine, j]]

    def shrink_part():
        for k in range(1, nb):
            a_send(k).wait()
        total = jnp.zeros((rank, x_v.shape[0]), jnp.float32)
        for h in range(nb):
            every = lax.dot_general(
                a_tab[h].reshape(half * rank, a_tab.shape[3]), x_v[...],
                (((1,), (1,)), ((), ())), preferred_element_type=jnp.float32,
            )
            for j in range(half):
                here = slot_ref[...] == h * cap + rep * half + j
                total += jnp.where(here, every[j * rank:(j + 1) * rank], 0.0)
        rr = rank // nd
        for p in range(nd):
            rs_snd[p] = total[p * rr:(p + 1) * rr]

        def go(k, carry):
            rs_send(k).start()
            return carry

        lax.fori_loop(1, nd, go, 0)

    def shrink_sum():
        all_small(rs_rcv, 0).wait()
        total = rs_snd[lin]
        for k in range(nd - 1):
            total += rs_rcv[k]
        ag[lin] = total.astype(jnp.bfloat16).astype(jnp.float32)

        def go(k, carry):
            ag_send(k).start()
            return carry

        lax.fori_loop(1, nd, go, 0)

    def decoded(d, t):
        for copy in sends(t, d):
            copy.wait_recv()
        return rcv[d, t].astype(jnp.int32).astype(jnp.float32) * rcv_scale[d, t]

    def step(t, carry):
        fetch(t + AHEAD)

        @pl.when(t < chunks)
        def _():
            w_copy(me * chunks + t).start()

        @pl.when(t == 0)
        def _():
            b_copy.start()

        for d in range(2):
            @pl.when(t < counts[d])
            def _():
                q = chunk_of(t, d)
                w_copy(q).wait()
                acc[0] = jnp.dot(x_v[...], w_v[q], preferred_element_type=jnp.float32)

                @pl.when(me > 0 if d == 0 else me < n - 1)
                def _():
                    acc[0] += decoded(d, t)

                @pl.when(t >= DEPTH)
                def _():
                    for copy in sends(t - DEPTH, d):
                        copy.wait_send()

                value = acc[0]
                most = jnp.maximum(jnp.max(jnp.abs(value), axis=0, keepdims=True), 1e-30)
                code = jnp.round(value * (TOP / most))
                snd[d, t % DEPTH] = code.astype(jnp.int32).astype(jnp.int16)
                snd_scale[d, t % DEPTH] = most * (1.0 / TOP)
                for copy in sends(t, d):
                    copy.start()

        for at, stage in ((1, pick_down), (2, pick_up), (steps // 2, shrink_part), (2 * steps // 3, shrink_sum)):
            pl.when(t == at)(stage)
        return carry

    lax.fori_loop(0, steps, step, 0)

    all_small(ag, 2).wait()
    low = ag[...].reshape(rank, x_v.shape[0])
    for s in range(nb * cap):
        here = slot_ref[...] == s
        spread[s * rank:(s + 1) * rank] = jnp.where(here, low, 0.0).astype(jnp.bfloat16)
    for k in range(1, nb):
        b_send(k).wait()
    for c in range(chunks):
        w_copy(me * chunks + c).wait()
        table = b_tab[:, :, :, c * cw:(c + 1) * cw].reshape(nb * cap * rank, cw)
        acc[c] = jnp.dot(
            x_v[...], w_v[me * chunks + c], preferred_element_type=jnp.float32
        ) + 0.5 * lax.dot_general(
            spread[...], table, (((0,), (0,)), ((), ())), preferred_element_type=jnp.float32
        )
    for c in range(chunks):
        for d in range(2):
            @pl.when(me > 0 if d == 0 else me < n - 1)
            def _():
                acc[c] += decoded(d, counts[d] + c)
        out_ref[:, c * cw:(c + 1) * cw] = acc[c].astype(out_ref.dtype)

    for d in range(2):
        def drain(t, carry):
            for copy in sends(t, d):
                copy.wait_send()
            return carry

        lax.fori_loop(jnp.maximum(counts[d] - DEPTH, 0), counts[d], drain, 0)


def solution(mesh):
    n, reps, nb = mesh.shape["mp"], mesh.shape["rep"], mesh.shape["batch"]

    def per_device(x, w, down, up, lists, slots):
        rows, depth = x.shape
        adapters, _, rank = down.shape
        width = up.shape[2]
        cap = lists.shape[2]
        half = cap // reps
        cw = min(256, width)
        chunks = width // cw
        steps = (n - 1) * chunks
        nd = n * reps
        bf, f32 = jnp.bfloat16, jnp.float32
        dma = pltpu.SemaphoreType.DMA
        hbm = pl.BlockSpec(memory_space=pl.ANY)
        vmem = pl.BlockSpec(memory_space=pltpu.VMEM)
        return pl.pallas_call(
            functools.partial(kernel, n, reps, nb, cw),
            out_shape=jax.ShapeDtypeStruct((rows, width), bf),
            in_specs=[hbm] * 4 + [pl.BlockSpec(memory_space=pltpu.SMEM), vmem],
            out_specs=vmem,
            scratch_shapes=[
                pltpu.VMEM((rows, depth), bf),
                pltpu.VMEM((n * chunks, depth, cw), bf),
                pltpu.VMEM((adapters, rank, depth), bf),
                pltpu.VMEM((adapters, rank, width), bf),
                pltpu.VMEM((nb - 1, half, rank, depth), bf),
                pltpu.VMEM((nb, half, rank, depth), bf),
                pltpu.VMEM((nb - 1, cap, rank, width), bf),
                pltpu.VMEM((nb, cap, rank, width), bf),
                pltpu.VMEM((2, DEPTH, rows, cw), jnp.int16),
                pltpu.VMEM((2, DEPTH, 1, cw), f32),
                pltpu.VMEM((2, steps, rows, cw), jnp.int16),
                pltpu.VMEM((2, steps, 1, cw), f32),
                pltpu.VMEM((nd, rank // nd, rows), f32),
                pltpu.VMEM((nd, rank // nd, rows), f32),
                pltpu.VMEM((nd, rank // nd, rows), f32),
                pltpu.VMEM((nb * cap * rank, rows), bf),
                pltpu.VMEM((chunks, rows, cw), f32),
                dma,
                dma((n * chunks,)),
                dma((2,)),
                dma((2, DEPTH)),
                dma((2, DEPTH)),
                dma((2, steps)),
                dma((2, steps)),
                dma((2, nb - 1)),
                dma((2, nb - 1)),
                dma((4,)),
            ],
            compiler_params=pltpu.CompilerParams(
                collective_id=0, has_side_effects=True, vmem_limit_bytes=56 * 1024 * 1024
            ),
            cost_estimate=pl.CostEstimate(
                flops=2 * rows * depth * w.shape[1], bytes_accessed=2 * w.size, transcendentals=0
            ),
        )(x, w, jnp.swapaxes(down, 1, 2), up, lists, slots.reshape(1, rows))

    in_specs = (
        P(("groups", "batch"), "mp"),
        P("mp", "rep"),
        P("batch", "mp", None),
        P("batch", None, ("rep", "mp")),
        P("groups", None, None),
        P(("groups", "batch")),
    )
    out_specs = P(("groups", "batch"), ("rep", "mp"))
    return jax.shard_map(
        per_device, mesh=mesh, in_specs=in_specs, out_specs=out_specs, check_vma=False
    )
```

time: 109 us -> 71.8 us (0.66)
  Pallas kernels: 0 us -> 69 us
  waiting for transfers between devices: 35.3 us -> 0 us
  blocking collectives: 24.9 us -> 0 us
  matrix products: 14.9 us -> 0 us
  between operations: 13.4 us -> 0.01 us
  local copies, waits for them, and re-layouts: 12.4 us -> 1.87 us
  starting transfers between devices: 7.92 us -> 0 us
    pallas_call x0 -> x1, Pallas kernels: none -> 69 us  [per_device(): pl.pallas_call(functools.partial(kernel, n, reps, nb, cw), out_shape=jax....]
    psum x1 -> x0, blocking collectives: 24.9 us -> none  [per_device(): shrink = lax.psum(partial_shrink, 'mp').astype(jnp.bfloat16)]
    all_to_all x2 -> x0, waiting for transfers between devices: 22.3 us -> none  [the longest x1 22.3 us: per_device(): lax.all_to_all(picked_down, 'batch', split_axis=0, concat_axis=0, tiled=T...]
    dot_general x3 -> x0, matrix products: 14.9 us -> none  [the longest x1 10.1 us: per_device(): jnp.dot(attention_input, output_weight_matrix, preferred_element_type=jnp...]
    reduce_scatter x1 -> x0, waiting for transfers between devices: 13 us -> none  [per_device(): summed = lax.psum_scatter(base, 'mp', scatter_dimension=1, tiled=True)]
    gather x2 -> x0, local copies, waits for them, and re-layouts: 9.17 us -> none  [the longest x1 5.37 us: per_device(): picked_down = down_factor_weights[wanted]]
    all_to_all x2 -> x0, starting transfers between devices: 7.92 us -> none  [the longest x1 4.34 us: per_device(): lax.all_to_all(picked_down, 'batch', split_axis=0, concat_axis=0, tiled=T...]
    unnamed x8 -> x1, local copies, waits for them, and re-layouts: 3.19 us -> 1.87 us
  transfers between devices with their start and end apart: 3 -> 0, of which waited for: 2 -> 0; matrix products, arithmetic and copies ran while one was open for 11% -> 0% of each run, Pallas kernels for 0% -> 0%
where the time goes in v1:
time: 71.8 us; the launch traced here: 70.9 us
  Pallas kernels  69 us (96%)
  local copies, waits for them, and re-layouts  1.87 us (3%)
    pallas_call x1, Pallas kernels, per_device(): pl.pallas_call(functools.partial(kernel, n, reps, nb, cw), out_shape=jax....  69 us
    unnamed x1, local copies, waits for them, and re-layouts  1.87 us

profile of v1, /device:TPU:0, one launch (start us, length us, event | category | flops | bytes accessed | tf_op | source)
XLA Modules:
  0.0 70.9 jit_solution(13752365873172424106)
XLA Ops:
  0.0 69.0 %shard_map.64 = bf16[256,1024]{1,0:T(8,128)(2,1)} custom-call(bf16[256,2048]{1,0:T(8,128)(2,1)} %x_hbm.1, bf16[2048,4096]{1,0:T(8,128)(2,1)} %w_hbm.1, bf16[32,64,2048]{2,1,0:T(8,128)(2,1)} %bitcast.2, bf16[32,64,1024]{2,1,0:T(8,128)(2,1)} %b_hbm.1, s32[2,2,4]{2,1,0:T(2,128)} %lists.1, s32[1,256]{1,0:T(1,128)} %bitcast.3), custom_call_target="tpu_custom_call" | custom-call | flops 4294967296 | bytes 16777216 | tf_op jit(solution)/shard_map/pallas_call | solution.py:270
  69.1 1.9 %copy.8 = bf16[256,1024]{1,0:T(8,128)(2,1)} copy(bf16[256,1024]{1,0:T(8,128)(2,1)} %shard_map.64) | data formatting | bytes 1048576

commit v2 on v1

--- a/solution.py
+++ b/solution.py
@@ -11,6 +11,8 @@
 TOP = 32766.0
 DEPTH = 2
 AHEAD = 2
+LAG = 2
+OWN = 0
 
 
 def kernel(
@@ -40,9 +42,11 @@
         s, c = t // chunks, t % chunks
         return ((n - 1 - s) if d == 0 else s) * chunks + c
 
-    def fetch(t):
+    def fetch(tick):
         for d in range(2):
-            @pl.when(t < counts[d])
+            t = tick - LAG * (me if d == 0 else n - 1 - me)
+
+            @pl.when((t >= 0) & (t < counts[d]))
             def _():
                 w_copy(chunk_of(t, d)).start()
 
@@ -178,25 +182,23 @@
             copy.wait_recv()
         return rcv[d, t].astype(jnp.int32).astype(jnp.float32) * rcv_scale[d, t]
 
-    def step(t, carry):
-        fetch(t + AHEAD)
-
-        @pl.when(t < chunks)
-        def _():
-            w_copy(me * chunks + t).start()
-
-        @pl.when(t == 0)
-        def _():
-            b_copy.start()
-
+    hops = (me, n - 1 - me)
+
+    def step(tick, carry):
         for d in range(2):
-            @pl.when(t < counts[d])
+            t = tick - LAG * hops[d]
+
+            @pl.when((t + AHEAD >= 0) & (t + AHEAD < counts[d]))
+            def _():
+                w_copy(chunk_of(t + AHEAD, d)).start()
+
+            @pl.when((t >= 0) & (t < counts[d]))
             def _():
                 q = chunk_of(t, d)
                 w_copy(q).wait()
                 acc[0] = jnp.dot(x_v[...], w_v[q], preferred_element_type=jnp.float32)
 
-                @pl.when(me > 0 if d == 0 else me < n - 1)
+                @pl.when(hops[d] > 0)
                 def _():
                     acc[0] += decoded(d, t)
 
@@ -213,11 +215,19 @@
                 for copy in sends(t, d):
                     copy.start()
 
+        @pl.when(tick == 0)
+        def _():
+            b_copy.start()
+
+        @pl.when((tick >= OWN) & (tick < OWN + chunks))
+        def _():
+            w_copy(me * chunks + tick - OWN).start()
+
         for at, stage in ((1, pick_down), (2, pick_up), (steps // 2, shrink_part), (2 * steps // 3, shrink_sum)):
-            pl.when(t == at)(stage)
+            pl.when(tick == at)(stage)
         return carry
 
-    lax.fori_loop(0, steps, step, 0)
+    lax.fori_loop(0, (n - 1) * max(chunks, LAG) + OWN, step, 0)
 
     all_small(ag, 2).wait()
     low = ag[...].reshape(rank, x_v.shape[0])

time: 71.8 us -> 46.6 us (0.65)
  Pallas kernels: 69 us -> 44.5 us
    pallas_call x1, Pallas kernels: 69 us -> 44.5 us  [per_device(): pl.pallas_call(functools.partial(kernel, n, reps, nb, cw), out_shape=jax....]
where the time goes in v2:
time: 46.6 us; the launch traced here: 46.4 us
  Pallas kernels  44.5 us (95%)
  local copies, waits for them, and re-layouts  1.87 us (4%)
    pallas_call x1, Pallas kernels, per_device(): pl.pallas_call(functools.partial(kernel, n, reps, nb, cw), out_shape=jax....  44.5 us
    unnamed x1, local copies, waits for them, and re-layouts  1.87 us

profile of v2, /device:TPU:0, one launch (start us, length us, event | category | flops | bytes accessed | tf_op | source)
XLA Modules:
  0.0 46.4 jit_solution(477120211381374034)
XLA Ops:
  0.0 44.5 %shard_map.64 = bf16[256,1024]{1,0:T(8,128)(2,1)} custom-call(bf16[256,2048]{1,0:T(8,128)(2,1)} %x_hbm.1, bf16[2048,4096]{1,0:T(8,128)(2,1)} %w_hbm.1, bf16[32,64,2048]{2,1,0:T(8,128)(2,1)} %bitcast.2, bf16[32,64,1024]{2,1,0:T(8,128)(2,1)} %b_hbm.1, s32[2,2,4]{2,1,0:T(2,128)} %lists.1, s32[1,256]{1,0:T(1,128)} %bitcast.3), custom_call_target="tpu_custom_call" | custom-call | flops 4294967296 | bytes 16777216 | tf_op jit(solution)/shard_map/pallas_call | solution.py:280
  44.5 1.9 %copy.8 = bf16[256,1024]{1,0:T(8,128)(2,1)} copy(bf16[256,1024]{1,0:T(8,128)(2,1)} %shard_map.64) | data formatting | bytes 1048576

commit v3 on v2

--- a/solution.py
+++ b/solution.py
@@ -53,12 +53,11 @@
     x_copy = pltpu.make_async_copy(x_hbm, x_v, x_sem)
     a_copy = pltpu.make_async_copy(a_hbm, a_all, ab_sem.at[0])
     b_copy = pltpu.make_async_copy(b_hbm, b_all, ab_sem.at[1])
+    barrier = pltpu.get_barrier_semaphore()
+
     x_copy.start()
     for t in range(AHEAD):
         fetch(t)
-    a_copy.start()
-
-    barrier = pltpu.get_barrier_semaphore()
 
     def peer(k):
         p = lax.rem(lin + k, nd)
@@ -74,8 +73,16 @@
         return carry
 
     lax.fori_loop(1, nd, greet, 0)
+    a_copy.start()
+    x_copy.wait()
+
+    @pl.when((me == 0) | (me == n - 1))
+    def _():
+        q = jnp.where(me == 0, (n - 1) * chunks, 0)
+        w_copy(q).wait()
+        acc[0] = jnp.dot(x_v[...], w_v[q], preferred_element_type=jnp.float32)
+
     pl.semaphore_wait(barrier, nd - 1 + nb - 1)
-    x_copy.wait()
 
     def sends(t, d):
         to = {"mp": me + 1 if d == 0 else me - 1}
@@ -195,8 +202,11 @@
             @pl.when((t >= 0) & (t < counts[d]))
             def _():
                 q = chunk_of(t, d)
-                w_copy(q).wait()
-                acc[0] = jnp.dot(x_v[...], w_v[q], preferred_element_type=jnp.float32)
+
+                @pl.when(tick > 0)
+                def _():
+                    w_copy(q).wait()
+                    acc[0] = jnp.dot(x_v[...], w_v[q], preferred_element_type=jnp.float32)
 
                 @pl.when(hops[d] > 0)
                 def _():

time: 46.6 us -> 46.1 us (0.989)
  no operation moved by 1% of the time
where the time goes in v3:
time: 46.1 us; the launch traced here: 45.9 us
  Pallas kernels  44.1 us (96%)
  local copies, waits for them, and re-layouts  1.87 us (4%)
    pallas_call x1, Pallas kernels, per_device(): pl.pallas_call(functools.partial(kernel, n, reps, nb, cw), out_shape=jax....  44.1 us
    unnamed x1, local copies, waits for them, and re-layouts  1.87 us

profile of v3, /device:TPU:0, one launch (start us, length us, event | category | flops | bytes accessed | tf_op | source)
XLA Modules:
  0.0 45.9 jit_solution(18128130937575866997)
XLA Ops:
  0.0 44.1 %shard_map.64 = bf16[256,1024]{1,0:T(8,128)(2,1)} custom-call(bf16[256,2048]{1,0:T(8,128)(2,1)} %x_hbm.1, bf16[2048,4096]{1,0:T(8,128)(2,1)} %w_hbm.1, bf16[32,64,2048]{2,1,0:T(8,128)(2,1)} %bitcast.2, bf16[32,64,1024]{2,1,0:T(8,128)(2,1)} %b_hbm.1, s32[2,2,4]{2,1,0:T(2,128)} %lists.1, s32[1,256]{1,0:T(1,128)} %bitcast.3), custom_call_target="tpu_custom_call" | custom-call | flops 4294967296 | bytes 16777216 | tf_op jit(solution)/shard_map/pallas_call | solution.py:290
  44.1 1.9 %copy.8 = bf16[256,1024]{1,0:T(8,128)(2,1)} copy(bf16[256,1024]{1,0:T(8,128)(2,1)} %shard_map.64) | data formatting | bytes 1048576
